TPU v7x, 256 devices: a whole 4x4x8 slice. The times are simulated.
256 devices in a mesh: wide: 32 (over z, y), narrow: 8 (over x, core).
Axes of the slice: x: 4, y: 4, z: 8, core: 2. Of those that a mesh axis runs over, the one named last changes fastest.
Arguments:
- snapshots: float32 [1048576, 512], P(('wide', 'narrow')), may hold values from -300 to 300
- test_matrix: float32 [512, 128], replicated, may hold values from -0.25 to 0.25
Outputs:
- basis: float32 [1048576, 128], P(('wide', 'narrow'))
- coefficients: float32 [128, 512], replicated
All inputs are finite; a program needn't handle non-finite values.
Results may differ from a plain program's by a relative error of at most 0.000092.
Values sent between devices are 32-bit elements; how exact they have to be, the bound alone decides.
A program may use at most 64 MiB of HBM per device.

v0:
```python
import jax
import jax.numpy as jnp
from jax import lax
from jax.sharding import PartitionSpec as P


def on_device(snapshots, test_matrix):
    hi = lax.Precision.HIGHEST
    rank_cols = test_matrix.shape[1]
    total_rows = snapshots.shape[0] * lax.axis_size(("wide", "narrow"))
    scale = jnp.sqrt(jnp.float32(total_rows))
    identity = jnp.eye(rank_cols, dtype=jnp.float32)
    sketch = jnp.dot(snapshots, test_matrix, precision=hi, preferred_element_type=jnp.float32)
    gram = jnp.dot(sketch.T, sketch, precision=hi, preferred_element_type=jnp.float32)
    gram = lax.psum(gram, ("wide", "narrow"))
    lower = jnp.linalg.cholesky(gram)
    inverse = lax.linalg.triangular_solve(lower, identity, left_side=True, lower=True)
    ortho = jnp.dot(sketch, inverse.T, precision=hi, preferred_element_type=jnp.float32)
    partial_terms = jnp.dot(ortho.T, snapshots, precision=hi, preferred_element_type=jnp.float32)
    coefficients = lax.psum(partial_terms, ("wide", "narrow")) / scale
    return (ortho * scale, coefficients)


def solution(mesh):
    return jax.shard_map(
        on_device,
        mesh=mesh,
        in_specs=(P(("wide", "narrow"), None), P()),
        out_specs=(P(("wide", "narrow"), None), P()),
        check_vma=False,
    )
```

profile of v0, /device:TPU:1, one launch (start us, length us, event | category | flops | bytes accessed | tf_op | source)
XLA Modules:
  0.0 553.7 jit_solution(3847002441918551760)
XLA Ops:
  7.2 0.0 copy-start
  7.2 0.0 all-reduce.3.cloned.1.call-start
  7.2 0.9 copy-done
  8.1 9.1 %fusion.4 = f32[4096,128]{1,0:T(8,128)S(1)} fusion(f32[4096,512]{1,0:T(8,128)} %param.2, f32[512,128]{1,0:T(8,128)S(1)} %copy-done), kind=kOutput, calls=%fused_computation.12 | convolution fusion | flops 3221225472 | bytes 10747904 | tf_op jit(solution)/shard_map/dot_general | solution.py:13
  17.2 4.1 fusion.5
  21.3 0.0 all-reduce.3.cloned.1.call-update
  21.4 0.2 all-reduce.5.cloned.1.call-start
  21.6 241.8 %all-reduce.3.cloned.1.call-done = f32[128,128]{0,1:T(8,128)} async-done(((f32[128,128]{0,1:T(8,128)}), f32[128,128]{0,1:T(8,128)}) %all-reduce.3.cloned.1.call-update) | async-done | bytes 65552 | tf_op jit(solution)/shard_map/psum | solution.py:15
  263.4 0.9 copy.5
  264.4 0.9 fusion.3
  265.2 11.7 %cholesky.17 = f32[128,128]{1,0:T(8,128)S(1)} custom-call(f32[128,128]{1,0:T(8,128)S(1)} %fusion.3), custom_call_target="Cholesky" | custom-call | tf_op jit(solution)/shard_map/jit(cholesky)/cholesky | solution.py:16
  277.0 0.6 compare_reduce_fusion
  277.6 0.7 fusion
  278.3 9.8 %custom-call.6 = f32[1,128,128]{1,2,0:T(8,128)S(1)} custom-call(f32[1,128,128]{2,1,0:T(8,128)S(1)} %fusion), custom_call_target="InvertDiagBlocksLowerTriangular" | custom-call | tf_op jit(solution)/shard_map/triangular_solve | solution.py:17
  288.1 0.2 fusion.1
  288.3 3.1 broadcast_multiply_fusion
  291.5 8.5 %fusion.6 = f32[128,512]{1,0:T(8,128)} fusion(f32[4096,128]{1,0:T(8,128)S(1)} %get-tuple-element.3, f32[4096,512]{1,0:T(8,128)} %param.2), kind=kOutput, calls=%fused_computation.14 | convolution fusion | flops 3221225472 | bytes 10747904 | tf_op jit(solution)/shard_map/dot_general | solution.py:19
  300.0 0.0 all-reduce.5.cloned.1.call-update
  300.0 245.2 %all-reduce.5.cloned.1.call-done = f32[128,512]{1,0:T(8,128)} async-done(((f32[128,512]{1,0:T(8,128)}), f32[128,512]{1,0:T(8,128)}) %all-reduce.5.cloned.1.call-update) | async-done | bytes 262160 | tf_op jit(solution)/shard_map/psum | solution.py:20
  545.2 1.7 broadcast_multiply_fusion.1
  (1 shorter events, 0.0 us)
Async XLA Ops:
  7.2 1.0 copy-start
  7.2 256.3 %all-reduce.3.cloned.1.call-start = ((), (), s32[]{:S(2)}) async-start(), calls=%async_computation | async-start | bytes 131072 | tf_op jit(solution)/shard_map/psum | solution.py:15
  21.4 523.9 %all-reduce.5.cloned.1.call-start = ((), (), s32[]{:S(2)}) async-start(), calls=%async_computation.1 | async-start | bytes 524288 | tf_op jit(solution)/shard_map/psum | solution.py:20
Sparse Core Ops, SparseCore 0:
  21.5 241.9 all-reduce.2
  300.1 245.0 all-reduce.4
where the time goes:
time: 555 us; the launch traced here: 554 us
  waiting for transfers between devices  487 us (88%)
  other arithmetic  25.4 us (5%)
  matrix products  25.1 us (5%)
  between operations  14.1 us (3%)
    psum x1, waiting for transfers between devices, on_device(): coefficients = lax.psum(partial_terms, ('wide', 'narrow')) / scale  245 us
    psum x1, waiting for transfers between devices, on_device(): gram = lax.psum(gram, ('wide', 'narrow'))  242 us
    another operation x3, other arithmetic, on_device(): lower = jnp.linalg.cholesky(gram)  12.4 us
  transfers between devices with their start and end apart: 2, of which 2 were waited for; matrix products, arithmetic and copies ran while one was open for 0% of the time, Pallas kernels for 0%

commit v1 on v0

v1 whole, which is shorter than its diff:
```python
import functools
import math

import jax
import jax.numpy as jnp
from jax import lax
from jax.experimental import pallas as pl
from jax.experimental.pallas import tpu as pltpu
from jax.sharding import PartitionSpec as P

MESH = pl.DeviceIdType.MESH
ROW = 4
SHARES = (1, 2, 3, 4, 6)
PANEL = 8
TURNS = (0, 0)
F32 = jnp.float32
BF16 = jnp.bfloat16


def halves(x):
    high = x.astype(BF16)
    return high, (x - high.astype(F32)).astype(BF16)


def dot(a, b, dims=((1,), (0,))):
    return lax.dot_general(a, b, (dims, ((), ())), preferred_element_type=F32)


def flips(index, size):
    steps, unit = [0], 1
    while unit < size:
        step = (1 - 2 * lax.rem(index // unit, 2)) * unit
        steps += [step + s for s in steps]
        unit *= 2
    return steps


def inverse_factor(g):
    n = g.shape[0]
    row = lax.broadcasted_iota(jnp.int32, (n, n), 0)
    col = lax.broadcasted_iota(jnp.int32, (n, n), 1)
    w = jnp.where(row == col, F32(1), F32(0))
    at = lax.broadcasted_iota(jnp.int32, (PANEL, n), 0)
    for first in range(0, n, PANEL):
        columns = [jnp.broadcast_to(g[:, first + k:first + k + 1], g.shape) for k in range(PANEL)]
        top = [c[:PANEL] for c in columns]
        rest = [c[PANEL:] for c in columns]
        g_top, w_top = g[:PANEL], w[:PANEL]
        steps = []
        panel = jnp.zeros((PANEL, n), F32)
        for i in range(PANEL):
            r = lax.rsqrt(top[i][i:i + 1])
            u, v = g_top[i:i + 1] * r, w_top[i:i + 1] * r
            m = top[i] * r
            ahead = {}
            for k in range(i + 1, PANEL):
                ahead[k] = top[k][i:i + 1] * r
                top[k] = top[k] - m * ahead[k]
            if i + 1 < PANEL:
                g_top, w_top = g_top - m * u, w_top - m * v
            panel = jnp.where(at == i, v, panel)
            steps.append((r, u, v, ahead))
        if first + PANEL < n:
            g, w = g[PANEL:], w[PANEL:]
            for i, (r, u, v, ahead) in enumerate(steps):
                m = rest[i] * r
                for k in ahead:
                    rest[k] = rest[k] - m * ahead[k]
                g, w = g - m * u, w - m * v
        yield panel


class Exchange:
    def __init__(self, place, mine, into, slots, whole, send_sem, recv_sem):
        self.me, self.z, self.in_plane, self.along_z = place
        self.mine, self.into, self.slots, self.whole = mine, into, slots, whole
        self.send_sem, self.recv_sem = send_sem, recv_sem

    def send(self, src, dst, where, phase):
        pltpu.make_async_remote_copy(
            src_ref=src, dst_ref=dst, send_sem=self.send_sem.at[phase], recv_sem=self.recv_sem.at[phase],
            device_id=where, device_id_type=MESH,
        ).start()

    def settle(self, ref, sem):
        pltpu.make_async_copy(ref, ref, sem).wait()

    def scatter(self):
        for d, (t, where) in enumerate(self.in_plane):
            self.send(self.mine.at[t], self.into.at[d], where, 0)

    def across(self):
        self.settle(self.into, self.recv_sem.at[0])
        self.slots[self.z] = self.mine[self.me] + jnp.sum(self.into[...], axis=0)
        for where in self.along_z:
            self.send(self.slots.at[self.z], self.slots.at[self.z], where, 1)

    def gather(self):
        self.settle(self.slots.at[pl.ds(0, len(self.along_z))], self.recv_sem.at[1])
        self.whole[self.me] = jnp.sum(self.slots[...], axis=0)
        for _, where in self.in_plane:
            self.send(self.whole.at[self.me], self.whole.at[self.me], where, 2)

    def arrived(self):
        self.settle(self.into, self.recv_sem.at[2])

    def sent(self):
        self.settle(self.into, self.send_sem.at[0])
        self.settle(self.slots.at[pl.ds(0, len(self.along_z))], self.send_sem.at[1])
        self.settle(self.into, self.send_sem.at[2])


def reduce_kernel(
    plane, depth, lines,
    a_hbm, omega_hbm, basis_ref, inverse_ref, proj_ref,
    a, omega, s, sl, xt, ah, al, g_full,
    g_mine, g_in, g_z, g_all, p_mine, p_in, p_z, p_all,
    load_sem, g_send, g_recv, p_send, p_recv,
):
    rank, snaps = omega.shape[1], a.shape[1]
    unit = a.shape[0] // sum(SHARES)
    ends = [unit * sum(SHARES[:i + 1]) for i in range(len(SHARES))]
    chunks = [pl.ds(e - unit * n, unit * n) for e, n in zip(ends, SHARES)]

    load_omega = pltpu.make_async_copy(omega_hbm, omega, load_sem.at[len(chunks)])
    loads = [pltpu.make_async_copy(a_hbm.at[c], a.at[c], load_sem.at[i]) for i, c in enumerate(chunks)]
    for copy in [load_omega] + loads:
        copy.start()

    wide, narrow = lax.axis_index("wide"), lax.axis_index("narrow")
    z, me = wide // ROW, lax.rem(wide, ROW) * lines + narrow
    by_line = flips(narrow, lines)
    by_row = flips(lax.rem(wide, ROW), ROW)
    by_z = flips(z, depth)
    in_plane = [
        (me + r * lines + n, (wide + r, narrow + n)) for r in by_row for n in by_line
    ][1:]
    along_z = [(wide + d * ROW, narrow) for d in by_z][1:]

    barrier = pltpu.get_barrier_semaphore()
    for where in [w for _, w in in_plane] + along_z:
        pl.semaphore_signal(barrier, inc=1, device_id=where, device_id_type=MESH)

    place = me, z, in_plane, along_z
    gram = Exchange(place, g_mine, g_in, g_z, g_all, g_send, g_recv)
    parts = [
        Exchange(place, *(r.at[h] for r in (p_mine, p_in, p_z, p_all, p_send, p_recv))) for h in range(p_mine.shape[0])
    ]

    load_omega.wait()
    oh, ol = halves(omega[...])
    both = jnp.concatenate([oh, ol], axis=1)

    def gram_of(c):
        x_high, x_low = halves(s[c, :])
        x_t = x_high.T
        xt[:rank, c] = x_t
        sl[c, :] = x_low
        return dot(x_t, jnp.concatenate([x_high, x_low], axis=1))

    total = None
    for i in range(len(chunks) + 1):
        if i < len(chunks):
            c = chunks[i]
            loads[i].wait()
            high, low = halves(a[c, :])
            ah[c, :] = high
            al[c, :] = low
            w = dot(high, both)
            s[c, :] = w[:, :rank] + w[:, rank:] + dot(low, oh)
        if i > 0:
            term = gram_of(chunks[i - 1])
            total = term if total is None else total + term
    cross = total[:, rank:]
    g_full[...] = total[:, :rank] + cross + cross.T
    for t in range(plane):
        g_mine[t] = g_full[t * (rank // plane):(t + 1) * (rank // plane), :]
    pl.semaphore_wait(barrier, plane + depth - 2)
    gram.scatter()

    xt[rank:, :] = sl[...].T
    span = snaps // len(parts)
    tall = p_mine.shape[2]
    per = rank // tall
    for h, part in enumerate(parts):
        columns = slice(h * span, (h + 1) * span)
        w = dot(xt[...], ah[:, columns])
        proj = w[:rank] + w[rank:] + dot(xt[:rank, :], al[:, columns])
        for b in range(span // 128):
            part.mine[b * per:(b + 1) * per] = proj[:, b * 128:(b + 1) * 128].reshape(per, tall, 128)
        part.scatter()
    gram.across()
    for part in parts:
        part.across()
    gram.gather()
    for h, part in enumerate(parts):
        if TURNS[h] == 0:
            part.gather()
    gram.arrived()
    for t in range(plane):
        g_full[t * (rank // plane):(t + 1) * (rank // plane), :] = g_all[t]

    for i, panel in enumerate(inverse_factor(g_full[...])):
        inverse_ref[i * PANEL:(i + 1) * PANEL, :] = panel
        for h, part in enumerate(parts):
            if TURNS[h] == i + 1:
                part.gather()
    inverse = inverse_ref[...]
    wh, wl = halves(inverse * math.sqrt(a.shape[0] * plane * depth))
    both_w = jnp.concatenate([jnp.concatenate([wh, wh], axis=1), jnp.concatenate([wl, wl], axis=1)], axis=0)
    for c in chunks:
        x = jnp.concatenate(halves(s[c, :]), axis=1)
        w = dot(x, both_w, ((1,), (1,)))
        basis_ref[c, :] = w[:, :rank] + w[:, rank:]

    gram.sent()
    for h, part in enumerate(parts):
        part.arrived()
        for b in range(span // 128):
            proj_ref[:, h * span + b * 128:h * span + (b + 1) * 128] = (
                part.whole[b * per:(b + 1) * per].reshape(rank, 128)
            )
        part.sent()


def finish_kernel(rows, basis, inverse_ref, proj_ref, basis_hbm, coef_hbm, coef, sem):
    save = pltpu.make_async_copy(basis, basis_hbm, sem.at[0])
    save.start()
    high, low = halves(inverse_ref[...] * (1.0 / math.sqrt(rows)))
    left = jnp.concatenate([high, low, high, low], axis=1)
    for b in range(0, proj_ref.shape[1], 128):
        ph, p_low = halves(proj_ref[:, b:b + 128])
        coef[:, b:b + 128] = dot(left, jnp.concatenate([ph, ph, p_low, p_low], axis=0))
    save_coef = pltpu.make_async_copy(coef, coef_hbm, sem.at[1])
    save_coef.start()
    save_coef.wait()
    save.wait()


def on_device(plane, depth, lines, snapshots, test_matrix):
    rows, snaps = snapshots.shape
    rank = test_matrix.shape[1]
    vmem = pl.BlockSpec(memory_space=pltpu.VMEM)
    hbm = pl.BlockSpec(memory_space=pltpu.HBM)
    parts = rank * snaps // 1024 // plane
    counts = (plane, plane - 1, depth, plane)
    basis, inverse, proj = pl.pallas_call(
        functools.partial(reduce_kernel, plane, depth, lines),
        out_shape=(
            pltpu.VMEM((rows, rank), F32),
            pltpu.VMEM((rank, rank), F32),
            pltpu.VMEM((rank, snaps), F32),
        ),
        in_specs=[hbm, hbm],
        out_specs=(vmem, vmem, vmem),
        scratch_shapes=[
            pltpu.VMEM((rows, snaps), F32),
            pltpu.VMEM((snaps, rank), F32),
            pltpu.VMEM((rows, rank), F32),
            pltpu.VMEM((rows, rank), BF16),
            pltpu.VMEM((2 * rank, rows), BF16),
            pltpu.VMEM((rows, snaps), BF16),
            pltpu.VMEM((rows, snaps), BF16),
            pltpu.VMEM((rank, rank), F32),
            *[pltpu.VMEM((n, rank // plane, rank), F32) for n in counts],
            *[pltpu.VMEM((parts, n, 8, 128), F32) for n in counts],
            pltpu.SemaphoreType.DMA((len(SHARES) + 1,)),
            pltpu.SemaphoreType.DMA((3,)),
            pltpu.SemaphoreType.DMA((3,)),
            pltpu.SemaphoreType.DMA((parts, 3)),
            pltpu.SemaphoreType.DMA((parts, 3)),
        ],
        compiler_params=pltpu.CompilerParams(
            collective_id=0, has_side_effects=True, vmem_limit_bytes=44 << 20
        ),
        name="reduced",
    )(*(pltpu.with_memory_space_constraint(x, pltpu.HBM) for x in (snapshots, test_matrix)))
    return pl.pallas_call(
        functools.partial(finish_kernel, rows * plane * depth),
        out_shape=(pltpu.HBM((rows, rank), F32), pltpu.HBM((rank, snaps), F32)),
        in_specs=[vmem, vmem, vmem],
        out_specs=(hbm, hbm),
        scratch_shapes=[pltpu.VMEM((rank, snaps), F32), pltpu.SemaphoreType.DMA((2,))],
        compiler_params=pltpu.CompilerParams(vmem_limit_bytes=16 << 20),
        name="finish",
    )(basis, inverse, proj)


def solution(mesh):
    wide, lines = mesh.shape["wide"], mesh.shape["narrow"]
    plane, depth = ROW * lines, wide // ROW
    return jax.shard_map(
        functools.partial(on_device, plane, depth, lines),
        mesh=mesh,
        in_specs=(P(("wide", "narrow"), None), P()),
        out_specs=(P(("wide", "narrow"), None), P()),
        check_vma=False,
    )
```

time: 555 us -> 32.9 us (0.06)
  waiting for transfers between devices: 487 us -> 0 us
  Pallas kernels: 0 us -> 32.2 us
  other arithmetic: 25.4 us -> 0 us
  matrix products: 25.1 us -> 0 us
  between operations: 14.1 us -> 0.64 us
    psum x2 -> x0, waiting for transfers between devices: 487 us -> none  [the longest x1 245 us: on_device(): coefficients = lax.psum(partial_terms, ('wide', 'narrow')) / scale]
    pallas_call x0 -> x2, Pallas kernels: none -> 32.2 us  [the longest x1 30.8 us: on_device(): pl.pallas_call(functools.partial(reduce_kernel, plane, depth, lines), out...]
    dot_general x4 -> x0, matrix products: 24.9 us -> none  [the longest x1 9.11 us: on_device(): jnp.dot(snapshots, test_matrix, precision=hi, preferred_element_type=jnp....]
    another operation x5 -> x0, other arithmetic: 22.9 us -> none  [the longest x3 12.4 us: on_device(): lower = jnp.linalg.cholesky(gram)]
  transfers between devices with their start and end apart: 2 -> 0, of which waited for: 2 -> 0; matrix products, arithmetic and copies ran while one was open for 0% -> 0% of each run, Pallas kernels for 0% -> 0%
where the time goes in v1:
time: 32.9 us
  Pallas kernels  32.2 us (98%)
  between operations  0.64 us (2%)
    pallas_call x1, Pallas kernels, on_device(): pl.pallas_call(functools.partial(reduce_kernel, plane, depth, lines), out...  30.8 us
    pallas_call x1, Pallas kernels, on_device(): pl.pallas_call(functools.partial(finish_kernel, rows * plane * depth), ou...  1.41 us

profile of v1, /device:TPU:1, one launch (start us, length us, event | category | flops | bytes accessed | tf_op | source)
XLA Modules:
  0.0 32.9 jit_solution(11004297487803534955)
XLA Ops:
  0.6 30.8 %reduced.1 = (f32[4096,128]{1,0:T(8,128)S(1)}, f32[128,128]{1,0:T(8,128)S(1)}, f32[128,512]{1,0:T(8,128)S(1)}) custom-call(f32[4096,512]{1,0:T(8,128)} %a_hbm.1, f32[512,128]{1,0:T(8,128)} %omega_hbm.1), custom_call_target="tpu_custom_call" | custom-call | tf_op jit(solution)/shard_map/reduced/pallas_call | solution.py:247
  31.4 1.4 %finish.1 = (f32[4096,128]{1,0:T(8,128)}, f32[128,512]{1,0:T(8,128)}) custom-call(f32[4096,128]{1,0:T(8,128)S(1)} %get-tuple-element.5.basis, f32[128,128]{1,0:T(8,128)S(1)} %get-tuple-element.6.inverse_ref, f32[128,512]{1,0:T(8,128)S(1)} %get-tuple-element.7.proj_ref), custom_call_target="tpu_custom_call" | custom-call | tf_op jit(solution)/shard_map/finish/pallas_call | solution.py:278

commit v2 on v1

--- a/solution.py
+++ b/solution.py
@@ -12,7 +12,8 @@
 ROW = 4
 SHARES = (1, 2, 3, 4, 6)
 PANEL = 8
-TURNS = (0, 0)
+EARLY = 4
+PIECES = 3
 F32 = jnp.float32
 BF16 = jnp.bfloat16
 
@@ -36,38 +37,61 @@
 
 
 def inverse_factor(g):
-    n = g.shape[0]
-    row = lax.broadcasted_iota(jnp.int32, (n, n), 0)
-    col = lax.broadcasted_iota(jnp.int32, (n, n), 1)
-    w = jnp.where(row == col, F32(1), F32(0))
-    at = lax.broadcasted_iota(jnp.int32, (PANEL, n), 0)
-    for first in range(0, n, PANEL):
-        columns = [jnp.broadcast_to(g[:, first + k:first + k + 1], g.shape) for k in range(PANEL)]
-        top = [c[:PANEL] for c in columns]
-        rest = [c[PANEL:] for c in columns]
-        g_top, w_top = g[:PANEL], w[:PANEL]
-        steps = []
-        panel = jnp.zeros((PANEL, n), F32)
-        for i in range(PANEL):
-            r = lax.rsqrt(top[i][i:i + 1])
-            u, v = g_top[i:i + 1] * r, w_top[i:i + 1] * r
-            m = top[i] * r
-            ahead = {}
-            for k in range(i + 1, PANEL):
-                ahead[k] = top[k][i:i + 1] * r
-                top[k] = top[k] - m * ahead[k]
-            if i + 1 < PANEL:
-                g_top, w_top = g_top - m * u, w_top - m * v
-            panel = jnp.where(at == i, v, panel)
-            steps.append((r, u, v, ahead))
-        if first + PANEL < n:
-            g, w = g[PANEL:], w[PANEL:]
-            for i, (r, u, v, ahead) in enumerate(steps):
-                m = rest[i] * r
-                for k in ahead:
-                    rest[k] = rest[k] - m * ahead[k]
-                g, w = g - m * u, w - m * v
-        yield panel
+    n, size = g.shape[0], PANEL
+    shape = (size, n)
+    h = g.reshape(n // size, size, n)
+    lane = lax.broadcasted_iota(jnp.int32, shape, 1)
+    at = lax.broadcasted_iota(jnp.int32, shape, 0)
+
+    def row(x, i):
+        return jnp.broadcast_to(x[i:i + 1], shape)
+
+    def columns(x, first):
+        return [jnp.broadcast_to(x[..., first + k:first + k + 1], x.shape) for k in range(size)]
+
+    block = columns(h[0], 0)
+    for first in range(0, n, size):
+        last = first + size == n
+        if not last:
+            rest = columns(h[1:], first)
+            later = columns(h[1], first + size)
+        u = {(i, k): row(block[k], i) for i in range(size) for k in range(i, size)}
+        here = (lane >= first) & (lane < first + size)
+        top = jnp.where(here, jnp.where(lane == at + first, F32(1), F32(0)), h[0])
+        rows = [row(top, i) for i in range(size)]
+        scale = []
+        for i in range(size):
+            r = lax.rsqrt(u[i, i])
+            scale.append(r)
+            for k in range(i + 1, size):
+                u[i, k] = u[i, k] * r
+            for k in range(i + 1, size):
+                for m in range(k, size):
+                    u[k, m] = u[k, m] - u[i, k] * u[i, m]
+            rows[i] = rows[i] * r
+            for k in range(i + 1, size):
+                rows[k] = rows[k] - u[i, k] * rows[i]
+        panel = rows[0]
+        for i in range(1, size):
+            panel = jnp.where(at == i, rows[i], panel)
+        yield jnp.where(lane < first + size, panel, F32(0))
+        if not last:
+            h = jnp.where(here[None], F32(0), h[1:])
+            for i in range(size):
+                factor = rest[i] * scale[i][None]
+                near = factor[0]
+                for k in range(size):
+                    later[k] = later[k] - near * near[k:k + 1]
+                for k in range(i + 1, size):
+                    rest[k] = rest[k] - factor * u[i, k][None]
+                h = h - factor * rows[i][None]
+            block = later
+
+
+def basis_of(rows, weights):
+    rank = rows.shape[1]
+    w = dot(jnp.concatenate(halves(rows), axis=1), weights, ((1,), (1,)))
+    return w[:, :rank] + w[:, rank:]
 
 
 class Exchange:
@@ -112,8 +136,8 @@
 
 def reduce_kernel(
     plane, depth, lines,
-    a_hbm, omega_hbm, basis_ref, inverse_ref, proj_ref,
-    a, omega, s, sl, xt, ah, al, g_full,
+    a_hbm, omega_hbm, s, first_ref, weights_ref, left_ref, proj_ref,
+    a, omega, inverse_ref, sl, xt, ah, al, g_full,
     g_mine, g_in, g_z, g_all, p_mine, p_in, p_z, p_all,
     load_sem, g_send, g_recv, p_send, p_recv,
 ):
@@ -173,68 +197,69 @@
             total = term if total is None else total + term
     cross = total[:, rank:]
     g_full[...] = total[:, :rank] + cross + cross.T
-    for t in range(plane):
-        g_mine[t] = g_full[t * (rank // plane):(t + 1) * (rank // plane), :]
+    pieces = [slice(t * (rank // plane), (t + 1) * (rank // plane)) for t in range(plane)]
+    for t, piece in enumerate(pieces):
+        g_mine[t] = g_full[piece, :]
     pl.semaphore_wait(barrier, plane + depth - 2)
     gram.scatter()
 
     xt[rank:, :] = sl[...].T
     span = snaps // len(parts)
-    tall = p_mine.shape[2]
-    per = rank // tall
-    for h, part in enumerate(parts):
-        columns = slice(h * span, (h + 1) * span)
-        w = dot(xt[...], ah[:, columns])
-        proj = w[:rank] + w[rank:] + dot(xt[:rank, :], al[:, columns])
-        for b in range(span // 128):
-            part.mine[b * per:(b + 1) * per] = proj[:, b * 128:(b + 1) * 128].reshape(per, tall, 128)
-        part.scatter()
+    for first in range(0, snaps, 2 * span):
+        w = dot(xt[...], ah[:, first:first + 2 * span])
+        proj_ref[:, first:first + 2 * span] = (
+            w[:rank] + w[rank:] + dot(xt[:rank, :], al[:, first:first + 2 * span])
+        )
+        for q in (first // span, first // span + 1):
+            for t, piece in enumerate(pieces):
+                parts[q].mine[t] = proj_ref[piece, q * span:(q + 1) * span]
+            parts[q].scatter()
     gram.across()
     for part in parts:
         part.across()
     gram.gather()
-    for h, part in enumerate(parts):
-        if TURNS[h] == 0:
-            part.gather()
+    for part in parts:
+        part.gather()
     gram.arrived()
-    for t in range(plane):
-        g_full[t * (rank // plane):(t + 1) * (rank // plane), :] = g_all[t]
+    for t, piece in enumerate(pieces):
+        g_full[piece, :] = g_all[t]
 
     for i, panel in enumerate(inverse_factor(g_full[...])):
         inverse_ref[i * PANEL:(i + 1) * PANEL, :] = panel
-        for h, part in enumerate(parts):
-            if TURNS[h] == i + 1:
-                part.gather()
-    inverse = inverse_ref[...]
-    wh, wl = halves(inverse * math.sqrt(a.shape[0] * plane * depth))
-    both_w = jnp.concatenate([jnp.concatenate([wh, wh], axis=1), jnp.concatenate([wl, wl], axis=1)], axis=0)
-    for c in chunks:
-        x = jnp.concatenate(halves(s[c, :]), axis=1)
-        w = dot(x, both_w, ((1,), (1,)))
-        basis_ref[c, :] = w[:, :rank] + w[:, rank:]
+    inverse, scale = inverse_ref[...], math.sqrt(a.shape[0] * plane * depth)
+    wh, wl = halves(inverse * scale)
+    weights_ref[...] = jnp.concatenate(
+        [jnp.concatenate([wh, wh], axis=1), jnp.concatenate([wl, wl], axis=1)], axis=0
+    )
+    left_ref[...] = jnp.concatenate(halves(inverse * (1.0 / scale)) * 2, axis=1)
+    early = first_ref.shape[0]
+    first_ref[...] = basis_of(s[:early, :], weights_ref[...])
 
     gram.sent()
-    for h, part in enumerate(parts):
+    for q, part in enumerate(parts):
         part.arrived()
-        for b in range(span // 128):
-            proj_ref[:, h * span + b * 128:h * span + (b + 1) * 128] = (
-                part.whole[b * per:(b + 1) * per].reshape(rank, 128)
-            )
+        for t, piece in enumerate(pieces):
+            proj_ref[piece, q * span:(q + 1) * span] = part.whole[t]
         part.sent()
 
 
-def finish_kernel(rows, basis, inverse_ref, proj_ref, basis_hbm, coef_hbm, coef, sem):
-    save = pltpu.make_async_copy(basis, basis_hbm, sem.at[0])
-    save.start()
-    high, low = halves(inverse_ref[...] * (1.0 / math.sqrt(rows)))
-    left = jnp.concatenate([high, low, high, low], axis=1)
+def finish_kernel(s, first, weights, left, proj_ref, basis_hbm, coef_hbm, basis, coef, sem):
+    rows, early = s.shape[0], first.shape[0]
+    saves = [pltpu.make_async_copy(first, basis_hbm.at[pl.ds(0, early)], sem.at[0])]
+    saves[0].start()
+    span = (rows - early) // PIECES
+    for i in range(PIECES):
+        c = pl.ds(early + i * span, span)
+        basis[c, :] = basis_of(s[c, :], weights[...])
+        saves.append(pltpu.make_async_copy(basis.at[c], basis_hbm.at[c], sem.at[i + 1]))
+        saves[-1].start()
     for b in range(0, proj_ref.shape[1], 128):
         ph, p_low = halves(proj_ref[:, b:b + 128])
-        coef[:, b:b + 128] = dot(left, jnp.concatenate([ph, ph, p_low, p_low], axis=0))
-    save_coef = pltpu.make_async_copy(coef, coef_hbm, sem.at[1])
-    save_coef.start()
-    save_coef.wait()
-    save.wait()
+        coef[:, b:b + 128] = dot(left[...], jnp.concatenate([ph, ph, p_low, p_low], axis=0))
+    saves.append(pltpu.make_async_copy(coef, coef_hbm, sem.at[PIECES + 1]))
+    saves[-1].start()
+    for save in saves:
+        save.wait()
 
 
 def on_device(plane, depth, lines, snapshots, test_matrix):
@@ -242,28 +267,30 @@
     rank = test_matrix.shape[1]
     vmem = pl.BlockSpec(memory_space=pltpu.VMEM)
     hbm = pl.BlockSpec(memory_space=pltpu.HBM)
-    parts = rank * snaps // 1024 // plane
+    parts = snaps // rank
     counts = (plane, plane - 1, depth, plane)
-    basis, inverse, proj = pl.pallas_call(
+    results = pl.pallas_call(
         functools.partial(reduce_kernel, plane, depth, lines),
         out_shape=(
             pltpu.VMEM((rows, rank), F32),
-            pltpu.VMEM((rank, rank), F32),
+            pltpu.VMEM((rows // EARLY, rank), F32),
+            pltpu.VMEM((2 * rank, 2 * rank), BF16),
+            pltpu.VMEM((rank, 4 * rank), BF16),
             pltpu.VMEM((rank, snaps), F32),
         ),
         in_specs=[hbm, hbm],
-        out_specs=(vmem, vmem, vmem),
+        out_specs=(vmem,) * 5,
         scratch_shapes=[
             pltpu.VMEM((rows, snaps), F32),
             pltpu.VMEM((snaps, rank), F32),
-            pltpu.VMEM((rows, rank), F32),
+            pltpu.VMEM((rank, rank), F32),
             pltpu.VMEM((rows, rank), BF16),
             pltpu.VMEM((2 * rank, rows), BF16),
             pltpu.VMEM((rows, snaps), BF16),
             pltpu.VMEM((rows, snaps), BF16),
             pltpu.VMEM((rank, rank), F32),
             *[pltpu.VMEM((n, rank // plane, rank), F32) for n in counts],
-            *[pltpu.VMEM((parts, n, 8, 128), F32) for n in counts],
+            *[pltpu.VMEM((parts, n, rank // plane, rank), F32) for n in counts],
             pltpu.SemaphoreType.DMA((len(SHARES) + 1,)),
             pltpu.SemaphoreType.DMA((3,)),
             pltpu.SemaphoreType.DMA((3,)),
@@ -271,19 +298,23 @@
             pltpu.SemaphoreType.DMA((parts, 3)),
         ],
         compiler_params=pltpu.CompilerParams(
-            collective_id=0, has_side_effects=True, vmem_limit_bytes=44 << 20
+            collective_id=0, has_side_effects=True, vmem_limit_bytes=40 << 20
         ),
         name="reduced",
     )(*(pltpu.with_memory_space_constraint(x, pltpu.HBM) for x in (snapshots, test_matrix)))
     return pl.pallas_call(
-        functools.partial(finish_kernel, rows * plane * depth),
+        finish_kernel,
         out_shape=(pltpu.HBM((rows, rank), F32), pltpu.HBM((rank, snaps), F32)),
-        in_specs=[vmem, vmem, vmem],
+        in_specs=[vmem] * 5,
         out_specs=(hbm, hbm),
-        scratch_shapes=[pltpu.VMEM((rank, snaps), F32), pltpu.SemaphoreType.DMA((2,))],
+        scratch_shapes=[
+            pltpu.VMEM((rows, rank), F32),
+            pltpu.VMEM((rank, snaps), F32),
+            pltpu.SemaphoreType.DMA((PIECES + 2,)),
+        ],
         compiler_params=pltpu.CompilerParams(vmem_limit_bytes=16 << 20),
         name="finish",
-    )(basis, inverse, proj)
+    )(*results)
 
 
 def solution(mesh):

time: 32.9 us -> 32.4 us (0.985)
  Pallas kernels: 32.2 us -> 31.7 us
    pallas_call x1, Pallas kernels: 30.8 us -> 30 us  [on_device(): pl.pallas_call(functools.partial(reduce_kernel, plane, depth, lines), out...]
    pallas_call x1, Pallas kernels: 1.41 us -> 1.75 us  [on_device(): pl.pallas_call(finish_kernel, out_shape=(pltpu.HBM((rows, rank), F32), pl...]
where the time goes in v2:
time: 32.4 us
  Pallas kernels  31.7 us (98%)
  between operations  0.64 us (2%)
    pallas_call x1, Pallas kernels, on_device(): pl.pallas_call(functools.partial(reduce_kernel, plane, depth, lines), out...  30 us
    pallas_call x1, Pallas kernels, on_device(): pl.pallas_call(finish_kernel, out_shape=(pltpu.HBM((rows, rank), F32), pl...  1.75 us

profile of v2, /device:TPU:1, one launch (start us, length us, event | category | flops | bytes accessed | tf_op | source)
XLA Modules:
  0.0 32.4 jit_solution(10890056248230595678)
XLA Ops:
  0.6 30.0 %reduced.1 = (f32[4096,128]{1,0:T(8,128)S(1)}, f32[1024,128]{1,0:T(8,128)S(1)}, bf16[256,256]{1,0:T(8,128)(2,1)S(1)}, bf16[128,512]{1,0:T(8,128)(2,1)S(1)}, f32[128,512]{1,0:T(8,128)S(1)}) custom-call(f32[4096,512]{1,0:T(8,128)} %a_hbm.1, f32[512,128]{1,0:T(8,128)} %omega_hbm.1), custom_call_target="tpu_custom_call" | custom-call | tf_op jit(solution)/shard_map/reduced/pallas_call | solution.py:272
  30.6 1.8 %finish.1 = (f32[4096,128]{1,0:T(8,128)}, f32[128,512]{1,0:T(8,128)}) custom-call(f32[4096,128]{1,0:T(8,128)S(1)} %get-tuple-element.7.s, f32[1024,128]{1,0:T(8,128)S(1)} %get-tuple-element.8.first, bf16[256,256]{1,0:T(8,128)(2,1)S(1)} %get-tuple-element.9.weights, bf16[128,512]{1,0:T(8,128)(2,1)S(1)} %get-tuple-element.10.left, ...), custom_call_target="tpu_custom_call" | custom-call | tf_op jit(solution)/shard_map/finish/pallas_call | solution.py:305

commit v3 on v2

--- a/solution.py
+++ b/solution.py
@@ -13,7 +13,7 @@
 SHARES = (1, 2, 3, 4, 6)
 PANEL = 8
 EARLY = 4
-PIECES = 3
+PIECES = 6
 F32 = jnp.float32
 BF16 = jnp.bfloat16
 

time: 32.4 us -> 32.3 us (level)
  no operation moved by 1% of the time
where the time goes in v3:
time: 32.3 us
  Pallas kernels  31.6 us (98%)
  between operations  0.64 us (2%)
    pallas_call x1, Pallas kernels, on_device(): pl.pallas_call(functools.partial(reduce_kernel, plane, depth, lines), out...  30 us
    pallas_call x1, Pallas kernels, on_device(): pl.pallas_call(finish_kernel, out_shape=(pltpu.HBM((rows, rank), F32), pl...  1.64 us

profile of v3, /device:TPU:1, one launch (start us, length us, event | category | flops | bytes accessed | tf_op | source)
XLA Modules:
  0.0 32.3 jit_solution(1745725362035087450)
XLA Ops:
  0.6 30.0 %reduced.1 = (f32[4096,128]{1,0:T(8,128)S(1)}, f32[1024,128]{1,0:T(8,128)S(1)}, bf16[256,256]{1,0:T(8,128)(2,1)S(1)}, bf16[128,512]{1,0:T(8,128)(2,1)S(1)}, f32[128,512]{1,0:T(8,128)S(1)}) custom-call(f32[4096,512]{1,0:T(8,128)} %a_hbm.1, f32[512,128]{1,0:T(8,128)} %omega_hbm.1), custom_call_target="tpu_custom_call" | custom-call | tf_op jit(solution)/shard_map/reduced/pallas_call | solution.py:272
  30.6 1.6 %finish.1 = (f32[4096,128]{1,0:T(8,128)}, f32[128,512]{1,0:T(8,128)}) custom-call(f32[4096,128]{1,0:T(8,128)S(1)} %get-tuple-element.7.s, f32[1024,128]{1,0:T(8,128)S(1)} %get-tuple-element.8.first, bf16[256,256]{1,0:T(8,128)(2,1)S(1)} %get-tuple-element.9.weights, bf16[128,512]{1,0:T(8,128)(2,1)S(1)} %get-tuple-element.10.left, ...), custom_call_target="tpu_custom_call" | custom-call | tf_op jit(solution)/shard_map/finish/pallas_call | solution.py:305
